TPU v7x, 512 devices: a whole 4x4x16 slice. The times are simulated.
512 devices in a mesh: group: 8 (over x, core), dev: 64 (over z, y).
Axes of the slice: x: 4, y: 4, z: 16, core: 2. Of those that a mesh axis runs over, the one named last changes fastest.
Arguments:
- cam_jac: float32 [2, 9, 8, 262144], P(None, None, None, ('group', 'dev')), may hold values from -6 to 6
- lm_jac: float32 [2, 3, 8, 262144], P(None, None, None, ('group', 'dev')), may hold values from -6 to 6
- resid: float32 [2, 8, 262144], P(None, None, ('group', 'dev')), may hold values from -6 to 6
- cam_index: int32 [8, 262144], P(None, ('group', 'dev')), may hold values from 0 to 8191
Outputs:
- camera_step: float32 [9, 8192], P(None, 'dev')
- camera_residual: float32 [9, 8192], P(None, 'dev')
- landmark_step: float32 [3, 262144], P(None, ('group', 'dev'))
Inputs may be any that keep to these rules, and one draw needn't show every extreme that they name: `cam_index`: every observation names one of the 8192 cameras.
All inputs are finite; a program needn't handle non-finite values.
Results may differ from a plain program's by a relative error of at most 0.0003.
Values sent between devices are 32-bit elements; how exact they have to be, the bound alone decides.
A program may use at most 64 MiB of HBM per device.

v0:
```python
import jax
import jax.numpy as jnp
from jax import lax
from jax.sharding import PartitionSpec as P

CAM_DEV = 128
ITERS = 2
DAMPING = 1.0


def landmark_inverse(lm_jac):

    def entry(first, second):
        return jnp.sum(lm_jac[:, first] * lm_jac[:, second], axis=(0, 1))

    w_00 = entry(0, 0) + DAMPING
    w_11 = entry(1, 1) + DAMPING
    w_22 = entry(2, 2) + DAMPING
    w_01 = entry(0, 1)
    w_02 = entry(0, 2)
    w_12 = entry(1, 2)
    cof_00 = w_11 * w_22 - w_12 * w_12
    cof_01 = w_02 * w_12 - w_01 * w_22
    cof_02 = w_01 * w_12 - w_02 * w_11
    cof_11 = w_00 * w_22 - w_02 * w_02
    cof_12 = w_01 * w_02 - w_00 * w_12
    cof_22 = w_00 * w_11 - w_01 * w_01
    determinant = w_00 * cof_00 + w_01 * cof_01 + w_02 * cof_02
    rows = [
        jnp.stack([cof_00, cof_01, cof_02]),
        jnp.stack([cof_01, cof_11, cof_12]),
        jnp.stack([cof_02, cof_12, cof_22]),
    ]
    return jnp.stack(rows) / determinant[None, None]


def apply_inverse(inverse, vector):
    return jnp.sum(inverse * vector[None], axis=1)


def landmark_side(lm_jac, values):
    return jnp.sum(lm_jac * values[:, None], axis=(0, 2))


def back_project(lm_jac, landmark):
    return jnp.sum(lm_jac * landmark[None, :, None, :], axis=1)


def camera_apply(cam_jac, cam_values):
    return jnp.sum(cam_jac * cam_values[None], axis=1)


def camera_transpose(cam_jac, errors):
    return jnp.sum(cam_jac * errors[:, None], axis=0)


def to_cameras(values, cam_index, total_cams):
    flat_index = cam_index.reshape(-1)
    width = values.shape[0]

    def one_row(column):
        return jax.ops.segment_sum(column, flat_index, num_segments=total_cams)

    return jax.vmap(one_row)(values.reshape(width, -1))


def schur_obs(cam_jac, lm_jac, inverse, cam_values):
    applied = camera_apply(cam_jac, cam_values)
    landmark = apply_inverse(inverse, landmark_side(lm_jac, applied))
    return camera_transpose(cam_jac, applied - back_project(lm_jac, landmark))


def gather_cameras(tile):
    return lax.all_gather(tile, "dev", axis=1, tiled=True)


def reduce_cameras(terms):
    totals = lax.psum(terms, ("group", "dev"))
    width = terms.shape[1] // lax.axis_size("dev")
    return lax.dynamic_slice_in_dim(totals, lax.axis_index("dev") * width, width, 1)


def inner_product(left, right):
    return lax.psum(jnp.sum(left * right), "dev")


def body(cam_jac, lm_jac, resid, cam_index):
    total_cams = CAM_DEV * lax.axis_size("dev")
    inverse = landmark_inverse(lm_jac)
    land_rhs = apply_inverse(inverse, landmark_side(lm_jac, resid))
    errors = resid - back_project(lm_jac, land_rhs)
    stacked = jnp.concatenate(
        [camera_transpose(cam_jac, errors), jnp.sum(cam_jac * cam_jac, axis=0)], axis=0
    )
    summed = reduce_cameras(to_cameras(stacked, cam_index, total_cams))
    gradient = summed[:9]
    diagonal = summed[9:] + DAMPING
    residual = gradient
    precond = residual / diagonal
    direction = precond
    rz_now = inner_product(residual, precond)
    solution = jnp.zeros_like(gradient)
    for iteration in range(ITERS):
        whole = gather_cameras(direction)
        cam_values = jnp.take(whole, cam_index, axis=1)
        terms = to_cameras(schur_obs(cam_jac, lm_jac, inverse, cam_values), cam_index, total_cams)
        image = reduce_cameras(terms) + DAMPING * direction
        alpha = rz_now / inner_product(direction, image)
        solution = solution + alpha * direction
        residual = residual - alpha * image
        if iteration + 1 < ITERS:
            precond = residual / diagonal
            rz_next = inner_product(residual, precond)
            direction = precond + rz_next / rz_now * direction
            rz_now = rz_next
    whole_step = gather_cameras(solution)
    cam_obs = camera_apply(cam_jac, jnp.take(whole_step, cam_index, axis=1))
    landmark_step = land_rhs - apply_inverse(inverse, landmark_side(lm_jac, cam_obs))
    return (solution, residual, landmark_step)


def solution(mesh):
    in_specs = (
        P(None, None, None, ("group", "dev")),
        P(None, None, None, ("group", "dev")),
        P(None, None, ("group", "dev")),
        P(None, ("group", "dev")),
    )
    out_specs = (P(None, "dev"), P(None, "dev"), P(None, ("group", "dev")))
    return jax.shard_map(body, mesh=mesh, in_specs=in_specs, out_specs=out_specs, check_vma=False)
```

profile of v0, /device:TPU:8, one launch (start us, length us, event | category | flops | bytes accessed | tf_op | source)
XLA Modules:
  0.0 2390.0 jit_solution(14837299796872105308)
XLA Ops:
  11.5 1.0 multiply_reduce_fusion.6
  13.2 24.5 %scatter_custom_fusion = f32[18,8192]{0,1:T(8,128)} fusion(s32[4096]{0:T(1024)S(1)} %bitcast.43, f32[4096,18]{1,0:T(8,128)S(1)} %bitcast.38, f32[]{:T(128)} %constant.14.clone.1), kind=kCustom, calls=%fused_computation.13 | custom fusion | flops 73728 | bytes 589828 | tf_op jit(solution)/shard_map/vmap()/scatter-add | solution.py:62
  37.9 494.2 %all-reduce.5.cloned.1.call-done = f32[18,8192]{0,1:T(8,128)} async-done(((f32[18,8192]{0,1:T(8,128)}), f32[18,8192]{0,1:T(8,128)}) %all-reduce.5.cloned.1.call-update) | async-done | bytes 589840 | tf_op jit(solution)/shard_map/psum | solution.py:78
  533.1 111.9 %all_gather.9 = f32[9,8192]{0,1:T(8,128)} all-gather(f32[9,128]{0,1:T(8,128)S(1)} %fusion.7), channel_id=1, replica_groups=mesh['group'=8,'dev'=64] {'dev'}, dimensions={1}, use_global_device_ids=true | all-gather | bytes 299520 | tf_op jit(solution)/shard_map/all_gather | solution.py:74
  645.0 16.3 gather_fusion
  661.3 1.9 select_bitcast_fusion.2
  664.8 24.5 %scatter_custom_fusion.1 = f32[9,8192]{0,1:T(8,128)} fusion(s32[4096]{0:T(1024)S(1)} %bitcast.44, f32[4096,9]{1,0:T(8,128)S(1)} %bitcast.40, f32[]{:T(128)} %constant.14.clone.1), kind=kCustom, calls=%fused_computation.11 | custom fusion | flops 36864 | bytes 294916 | tf_op jit(solution)/shard_map/vmap()/scatter-add | solution.py:62
  689.4 488.0 %all-reduce.7.cloned.1.call-done = f32[9,8192]{0,1:T(8,128)} async-done(((f32[9,8192]{0,1:T(8,128)}), f32[9,8192]{0,1:T(8,128)}) %all-reduce.7.cloned.1.call-update) | async-done | bytes 294928 | tf_op jit(solution)/shard_map/psum | solution.py:78
  1177.4 1.6 multiply_reduce_fusion.16
  1179.0 139.5 %all-reduce = (f32[]{:T(128)}, f32[]{:T(128)}) all-reduce(f32[]{:T(128)} %get-tuple-element.22, f32[]{:T(128)} %get-tuple-element.21), channel_id=1, replica_groups=mesh['group'=8,'dev'=64] {'dev'}, use_global_device_ids=true, to_apply=%region_14.0 | all-reduce | flops 2 | bytes 16 | tf_op jit(solution)/shard_map/psum | solution.py:84
  1319.8 1.6 multiply_reduce_fusion.15
  1321.4 140.7 %psum.53 = f32[]{:T(128)} all-reduce(f32[]{:T(128)} %get-tuple-element.25), channel_id=1, replica_groups=mesh['group'=8,'dev'=64] {'dev'}, use_global_device_ids=true, to_apply=%region_25.27 | all-reduce | flops 1 | bytes 8 | tf_op jit(solution)/shard_map/psum | solution.py:84
  1463.5 1.0 multiply_add_fusion.1
  1464.5 110.5 %all_gather.10 = f32[9,8192]{0,1:T(8,128)} all-gather(f32[9,128]{0,1:T(8,128)S(1)} %multiply_add_fusion.1), channel_id=1, replica_groups=mesh['group'=8,'dev'=64] {'dev'}, dimensions={1}, use_global_device_ids=true | all-gather | bytes 299520 | tf_op jit(solution)/shard_map/all_gather | solution.py:74
  1575.0 16.3 gather_fusion.1
  1591.2 1.9 select_bitcast_fusion.1
  1594.6 24.5 %scatter_custom_fusion.2 = f32[9,8192]{0,1:T(8,128)} fusion(s32[4096]{0:T(1024)S(1)} %bitcast.45, f32[4096,9]{1,0:T(8,128)S(1)} %bitcast.39, f32[]{:T(128)} %constant.14.clone.1), kind=kCustom, calls=%fused_computation.9 | custom fusion | flops 36864 | bytes 294916 | tf_op jit(solution)/shard_map/vmap()/scatter-add | solution.py:62
  1619.2 488.2 %all-reduce.9.cloned.1.call-done = f32[9,8192]{0,1:T(8,128)} async-done(((f32[9,8192]{0,1:T(8,128)}), f32[9,8192]{0,1:T(8,128)}) %all-reduce.9.cloned.1.call-update) | async-done | bytes 294928 | tf_op jit(solution)/shard_map/psum | solution.py:78
  2107.4 1.5 multiply_reduce_fusion.14
  2108.9 139.4 %psum.55 = f32[]{:T(128)} all-reduce(f32[]{:T(128)} %multiply_reduce_fusion.14), channel_id=1, replica_groups=mesh['group'=8,'dev'=64] {'dev'}, use_global_device_ids=true, to_apply=%region_34.36 | all-reduce | flops 1 | bytes 8 | tf_op jit(solution)/shard_map/psum | solution.py:84
  2249.7 1.0 multiply_subtract_fusion
  2251.4 111.8 %all_gather.11 = f32[9,8192]{0,1:T(8,128)} all-gather(f32[9,128]{0,1:T(8,128)S(1)} %get-tuple-element.34), channel_id=1, replica_groups=mesh['group'=8,'dev'=64] {'dev'}, dimensions={1}, use_global_device_ids=true | all-gather | bytes 299520 | tf_op jit(solution)/shard_map/all_gather | solution.py:74
  2363.9 16.3 gather_fusion.2
  2380.2 1.9 select_bitcast_fusion
  (50 shorter events, 11.6 us)
Async XLA Ops:
  7.2 524.9 %all-reduce.5.cloned.1.call-start = ((), (), s32[]{:S(2)}) async-start(), calls=%async_computation | async-start | bytes 8388608 | tf_op jit(solution)/shard_map/psum | solution.py:78
  13.2 24.6 %copy-start.2 = (s32[8,512]{1,0:T(8,128)S(1)}, s32[8,512]{1,0:T(8,128)}, u32[]{:S(2)}) copy-start(s32[8,512]{1,0:T(8,128)} %param.9) | copy-start | bytes 49156
  37.8 1139.6 %all-reduce.7.cloned.1.call-start = ((), (), s32[]{:S(2)}) async-start(), calls=%async_computation.1 | async-start | bytes 8388608 | tf_op jit(solution)/shard_map/psum | solution.py:78
  645.0 18.9 copy-start
  645.0 19.0 copy-start.1
  689.3 1418.1 %all-reduce.9.cloned.1.call-start = ((), (), s32[]{:S(2)}) async-start(), calls=%async_computation.2 | async-start | bytes 8388608 | tf_op jit(solution)/shard_map/psum | solution.py:78
Sparse Core Ops, SparseCore 0:
  37.9 494.1 all-reduce.4
  689.4 487.8 all-reduce.6
  1619.3 488.0 all-reduce.8
where the time goes:
time: 2390 us
  waiting for transfers between devices  1470 us (62%)
  blocking collectives  754 us (32%)
  other arithmetic  92.8 us (4%)
  local copies, waits for them, and re-layouts  54.8 us (2%)
    psum x3, waiting for transfers between devices, reduce_cameras(): totals = lax.psum(terms, ('group', 'dev'))  1470 us
    psum x3, blocking collectives, inner_product(): return lax.psum(jnp.sum(left * right), 'dev')  420 us
    all_gather x3, blocking collectives, gather_cameras(): return lax.all_gather(tile, 'dev', axis=1, tiled=True)  334 us
    scatter-add x3, other arithmetic, one_row(): return jax.ops.segment_sum(column, flat_index, num_segments=total_cams)  73.6 us
  transfers between devices with their start and end apart: 3, of which 3 were waited for; matrix products, arithmetic and copies ran while one was open for 0% of the time, Pallas kernels for 0%

commit v1 on v0

--- a/solution.py
+++ b/solution.py
@@ -75,7 +75,7 @@
 
 
 def reduce_cameras(terms):
-    totals = lax.psum(terms, ("group", "dev"))
+    totals = lax.psum(lax.psum(terms, "dev"), "group")
     width = terms.shape[1] // lax.axis_size("dev")
     return lax.dynamic_slice_in_dim(totals, lax.axis_index("dev") * width, width, 1)
 

time: 2390 us -> 2050 us (0.86)
  waiting for transfers between devices: 1470 us -> 1120 us
    psum x3 -> x6, waiting for transfers between devices: 1470 us -> 1120 us  [reduce_cameras(): totals = lax.psum(lax.psum(terms, 'dev'), 'group')]
  transfers between devices with their start and end apart: 3 -> 6, of which waited for: 3 -> 6; matrix products, arithmetic and copies ran while one was open for 0% -> 0% of each run, Pallas kernels for 0% -> 0%
where the time goes in v1:
time: 2050 us
  waiting for transfers between devices  1120 us (55%)
  blocking collectives  765 us (37%)
  other arithmetic  92.7 us (5%)
  local copies, waits for them, and re-layouts  54.8 us (3%)
    psum x6, waiting for transfers between devices, reduce_cameras(): totals = lax.psum(lax.psum(terms, 'dev'), 'group')  1120 us
    psum x3, blocking collectives, inner_product(): return lax.psum(jnp.sum(left * right), 'dev')  425 us
    all_gather x3, blocking collectives, gather_cameras(): return lax.all_gather(tile, 'dev', axis=1, tiled=True)  340 us
    scatter-add x3, other arithmetic, one_row(): return jax.ops.segment_sum(column, flat_index, num_segments=total_cams)  73.6 us
  transfers between devices with their start and end apart: 6, of which 6 were waited for; matrix products, arithmetic and copies ran while one was open for 0% of the time, Pallas kernels for 0%

profile of v1, /device:TPU:8, one launch (start us, length us, event | category | flops | bytes accessed | tf_op | source)
XLA Modules:
  0.0 2051.0 jit_solution(17932854570305599346)
XLA Ops:
  13.2 24.5 %scatter_custom_fusion = f32[18,8192]{0,1:T(8,128)} fusion(s32[4096]{0:T(1024)S(1)} %bitcast.43, f32[4096,18]{1,0:T(8,128)S(1)} %bitcast.38, f32[]{:T(128)} %constant.14.clone.1), kind=kCustom, calls=%fused_computation.13 | custom fusion | flops 73728 | bytes 589828 | tf_op jit(solution)/shard_map/vmap()/scatter-add | solution.py:62
  37.8 292.9 %all-reduce.8.cloned.1.call-done = f32[18,8192]{0,1:T(8,128)} async-done(((f32[18,8192]{0,1:T(8,128)}), f32[18,8192]{0,1:T(8,128)}) %all-reduce.8.cloned.1.call-update) | async-done | bytes 589840 | tf_op jit(solution)/shard_map/psum | solution.py:78
  330.8 86.4 %all-reduce.10.cloned.1.call-done = f32[18,8192]{0,1:T(8,128)} async-done(((f32[18,8192]{0,1:T(8,128)}), f32[18,8192]{0,1:T(8,128)}) %all-reduce.10.cloned.1.call-update) | async-done | bytes 589840 | tf_op jit(solution)/shard_map/psum | solution.py:78
  418.2 115.0 %all_gather.9 = f32[9,8192]{0,1:T(8,128)} all-gather(f32[9,128]{0,1:T(8,128)S(1)} %fusion.7), channel_id=1, replica_groups=mesh['group'=8,'dev'=64] {'dev'}, dimensions={1}, use_global_device_ids=true | all-gather | bytes 299520 | tf_op jit(solution)/shard_map/all_gather | solution.py:74
  533.2 16.3 gather_fusion
  549.5 1.9 select_bitcast_fusion.2
  553.0 24.5 %scatter_custom_fusion.1 = f32[9,8192]{0,1:T(8,128)} fusion(s32[4096]{0:T(1024)S(1)} %bitcast.44, f32[4096,9]{1,0:T(8,128)S(1)} %bitcast.40, f32[]{:T(128)} %constant.14.clone.1), kind=kCustom, calls=%fused_computation.11 | custom fusion | flops 36864 | bytes 294916 | tf_op jit(solution)/shard_map/vmap()/scatter-add | solution.py:62
  577.6 284.1 %all-reduce.12.cloned.1.call-done = f32[9,8192]{0,1:T(8,128)} async-done(((f32[9,8192]{0,1:T(8,128)}), f32[9,8192]{0,1:T(8,128)}) %all-reduce.12.cloned.1.call-update) | async-done | bytes 294928 | tf_op jit(solution)/shard_map/psum | solution.py:78
  861.8 86.3 %all-reduce.14.cloned.1.call-done = f32[9,8192]{0,1:T(8,128)} async-done(((f32[9,8192]{0,1:T(8,128)}), f32[9,8192]{0,1:T(8,128)}) %all-reduce.14.cloned.1.call-update) | async-done | bytes 294928 | tf_op jit(solution)/shard_map/psum | solution.py:78
  948.1 1.6 multiply_reduce_fusion.16
  949.7 140.8 %all-reduce = (f32[]{:T(128)}, f32[]{:T(128)}) all-reduce(f32[]{:T(128)} %get-tuple-element.22, f32[]{:T(128)} %get-tuple-element.21), channel_id=1, replica_groups=mesh['group'=8,'dev'=64] {'dev'}, use_global_device_ids=true, to_apply=%region_15.0 | all-reduce | flops 2 | bytes 16 | tf_op jit(solution)/shard_map/psum | solution.py:84
  1091.8 1.6 multiply_reduce_fusion.15
  1093.5 143.2 %psum.76 = f32[]{:T(128)} all-reduce(f32[]{:T(128)} %get-tuple-element.25), channel_id=1, replica_groups=mesh['group'=8,'dev'=64] {'dev'}, use_global_device_ids=true, to_apply=%region_27.29 | all-reduce | flops 1 | bytes 8 | tf_op jit(solution)/shard_map/psum | solution.py:84
  1239.1 110.6 %all_gather.10 = f32[9,8192]{0,1:T(8,128)} all-gather(f32[9,128]{0,1:T(8,128)S(1)} %multiply_add_fusion.1), channel_id=1, replica_groups=mesh['group'=8,'dev'=64] {'dev'}, dimensions={1}, use_global_device_ids=true | all-gather | bytes 299520 | tf_op jit(solution)/shard_map/all_gather | solution.py:74
  1349.7 16.3 gather_fusion.1
  1365.9 1.9 select_bitcast_fusion.1
  1369.3 24.5 %scatter_custom_fusion.2 = f32[9,8192]{0,1:T(8,128)} fusion(s32[4096]{0:T(1024)S(1)} %bitcast.45, f32[4096,9]{1,0:T(8,128)S(1)} %bitcast.39, f32[]{:T(128)} %constant.14.clone.1), kind=kCustom, calls=%fused_computation.9 | custom fusion | flops 36864 | bytes 294916 | tf_op jit(solution)/shard_map/vmap()/scatter-add | solution.py:62
  1394.0 283.7 %all-reduce.16.cloned.1.call-done = f32[9,8192]{0,1:T(8,128)} async-done(((f32[9,8192]{0,1:T(8,128)}), f32[9,8192]{0,1:T(8,128)}) %all-reduce.16.cloned.1.call-update) | async-done | bytes 294928 | tf_op jit(solution)/shard_map/psum | solution.py:78
  1677.7 86.3 %all-reduce.18.cloned.1.call-done = f32[9,8192]{0,1:T(8,128)} async-done(((f32[9,8192]{0,1:T(8,128)}), f32[9,8192]{0,1:T(8,128)}) %all-reduce.18.cloned.1.call-update) | async-done | bytes 294928 | tf_op jit(solution)/shard_map/psum | solution.py:78
  1764.0 1.5 multiply_reduce_fusion.14
  1765.5 140.8 %psum.79 = f32[]{:T(128)} all-reduce(f32[]{:T(128)} %multiply_reduce_fusion.14), channel_id=1, replica_groups=mesh['group'=8,'dev'=64] {'dev'}, use_global_device_ids=true, to_apply=%region_37.39 | all-reduce | flops 1 | bytes 8 | tf_op jit(solution)/shard_map/psum | solution.py:84
  1909.4 114.5 %all_gather.11 = f32[9,8192]{0,1:T(8,128)} all-gather(f32[9,128]{0,1:T(8,128)S(1)} %get-tuple-element.34), channel_id=1, replica_groups=mesh['group'=8,'dev'=64] {'dev'}, dimensions={1}, use_global_device_ids=true | all-gather | bytes 299520 | tf_op jit(solution)/shard_map/all_gather | solution.py:74
  2024.6 16.3 gather_fusion.2
  2040.8 1.9 select_bitcast_fusion
  (59 shorter events, 14.9 us)
Async XLA Ops:
  7.2 323.5 %all-reduce.8.cloned.1.call-start = ((), (), s32[]{:S(2)}) async-start(), calls=%async_computation | async-start | bytes 8388608 | tf_op jit(solution)/shard_map/psum | solution.py:78
  13.2 24.6 %copy-start.2 = (s32[8,512]{1,0:T(8,128)S(1)}, s32[8,512]{1,0:T(8,128)}, u32[]{:S(2)}) copy-start(s32[8,512]{1,0:T(8,128)} %param.9) | copy-start | bytes 49156
  37.7 379.5 %all-reduce.10.cloned.1.call-start = ((), (), s32[]{:S(2)}) async-start(), calls=%async_computation.1 | async-start | bytes 8388608 | tf_op jit(solution)/shard_map/psum | solution.py:78
  330.7 531.0 %all-reduce.12.cloned.1.call-start = ((), (), s32[]{:S(2)}) async-start(), calls=%async_computation.2 | async-start | bytes 8388608 | tf_op jit(solution)/shard_map/psum | solution.py:78
  533.2 18.9 copy-start
  533.2 19.0 copy-start.1
  577.5 370.5 %all-reduce.14.cloned.1.call-start = ((), (), s32[]{:S(2)}) async-start(), calls=%async_computation.3 | async-start | bytes 8388608 | tf_op jit(solution)/shard_map/psum | solution.py:78
  861.7 815.9 %all-reduce.16.cloned.1.call-start = ((), (), s32[]{:S(2)}) async-start(), calls=%async_computation.4 | async-start | bytes 8388608 | tf_op jit(solution)/shard_map/psum | solution.py:78
  1393.9 370.1 %all-reduce.18.cloned.1.call-start = ((), (), s32[]{:S(2)}) async-start(), calls=%async_computation.5 | async-start | bytes 8388608 | tf_op jit(solution)/shard_map/psum | solution.py:78
Sparse Core Ops, SparseCore 0:
  37.8 292.8 all-reduce.7
  333.0 84.0 all-reduce.9
  577.7 284.0 all-reduce.11
  863.9 84.0 all-reduce.13
  1394.0 283.6 all-reduce.15
  1679.9 84.0 all-reduce.17
